TPU v7x, 512 devices: a whole 4x8x8 slice. The times are simulated.
512 devices in a mesh: lon: 32 (over z_lo, y, core), lat: 4 (over z_hi), exp: 4 (over x).
Axes of the slice: x: 4, y: 8, z: 8 (z_hi: 4, z_lo: 2; z = z_hi * 2 + z_lo), core: 2. Of those that a mesh axis runs over, the one named last changes fastest.
Arguments:
- tokens: bfloat16 [8, 24, 384, 1024], P('exp', 'lat', 'lon'), may hold values from -6 to 6
- queries: bfloat16 [8, 24, 384, 1024], P('exp', 'lat', 'lon'), may hold values from -7 to 7
- keys: bfloat16 [8, 24, 384, 1024], P('exp', 'lat', 'lon'), may hold values from -7 to 7
- values: bfloat16 [8, 24, 384, 1024], P('exp', 'lat', 'lon'), may hold values from -24 to 24
- shift_lat: int32 [1], replicated, may hold values from 1 to 5
- shift_lon: int32 [1], replicated, may hold values from 1 to 11
- norm_gain: float32 [1024], replicated, may hold values from 0.5 to 2
- w_router: bfloat16 [1024, 32], replicated, may hold values from -0.1875 to 0.1875
- routes: int32 [4, 4, 32, 144, 2], P('exp', 'lat', 'lon'), may hold values from 0 to 31, all different within a row; in each aligned block of 144 rows (0 to 143, 144 to 287, ..., all dimensions but the last counted through in order) at most 12 rows name the same one
- w_gate: bfloat16 [32, 1024, 2048], P('lon', None, 'exp'), may hold values from -0.1875 to 0.1875
- w_up: bfloat16 [32, 1024, 2048], P('lon', None, 'exp'), may hold values from -0.1875 to 0.1875
- w_down: bfloat16 [32, 1024, 2048], P('lon', None, 'exp'), may hold values from -0.125 to 0.125
Outputs:
- layer_out: bfloat16 [8, 24, 384, 1024], P('exp', 'lat', 'lon')
Inputs may be any that keep to these rules, and one draw needn't show every extreme that they name: Each cell names two different experts. Among the 144 cells routes[i, j, m] no expert is named more than 12 times, and in some such block one is named exactly 12 times.
All inputs are finite; a program needn't handle non-finite values.
Results may differ from a plain program's by a relative error of at most 0.008.
Values may be sent and summed in bfloat16 or wider, within the bound.
A program may use at most 128 MiB of HBM per device.

v0:
```python
import jax
import jax.numpy as jnp
from jax import lax
from jax.sharding import PartitionSpec as P

HEAD_DIM = 32
WIN_LAT = 6
WIN_LON = 12


def with_halo(cells, sides, width):
    for axis, dim in sides:
        count = lax.axis_size(axis)
        head = lax.slice_in_dim(cells, 0, width, axis=dim)
        tail = lax.slice_in_dim(cells, cells.shape[dim] - width, cells.shape[dim], axis=dim)
        cells = jnp.concatenate(
            [
                lax.ppermute(tail, axis, [(i, (i + 1) % count) for i in range(count)]),
                cells,
                lax.ppermute(head, axis, [((i + 1) % count, i) for i in range(count)]),
            ],
            axis=dim,
        )
    return cells


def expert_hidden(row_block, gate_w, up_w):
    gate_act = jnp.einsum("secd,edf->secf", row_block, gate_w, preferred_element_type=jnp.float32)
    up_act = jnp.einsum("secd,edf->secf", row_block, up_w, preferred_element_type=jnp.float32)
    return (jax.nn.silu(gate_act) * up_act).astype(jnp.bfloat16)


def send_out(outgoing):
    return lax.all_to_all(outgoing, "lon", split_axis=0, concat_axis=0, tiled=True)


def send_back(results):
    return lax.all_to_all(results, "lon", split_axis=0, concat_axis=0, tiled=True)


def shards(
    tokens,
    queries,
    keys,
    values,
    shift_lat,
    shift_lon,
    norm_gain,
    w_router,
    routes,
    w_gate,
    w_up,
    w_down,
):
    levels_dev, rows_dev, cols_dev, width = tokens.shape
    heads = width // HEAD_DIM
    lon_wins = cols_dev // WIN_LON
    lat_shift = shift_lat[0]
    lon_shift = shift_lon[0]
    key_value = jnp.stack([keys, values]).reshape(
        2, levels_dev, 1, WIN_LAT, lon_wins, WIN_LON, width
    )
    framed = with_halo(key_value, (("lon", 4), ("lat", 2)), 1)
    framed = framed.reshape(2, levels_dev, 3 * WIN_LAT, (lon_wins + 2) * WIN_LON, width)
    zero_index = jnp.zeros((), jnp.int32)
    region = lax.dynamic_slice(
        framed,
        (zero_index, zero_index, WIN_LAT - lat_shift, WIN_LON - lon_shift, zero_index),
        (2, levels_dev, 2 * WIN_LAT, cols_dev + WIN_LON, width),
    )
    key_region = region[0].reshape(-1, heads, HEAD_DIM)
    value_region = region[1].reshape(-1, heads, HEAD_DIM)
    query_own = queries.reshape(-1, heads, HEAD_DIM)
    region_rows = jnp.arange(2 * WIN_LAT, dtype=jnp.int32)
    row_global = lax.axis_index("lat") * WIN_LAT + region_rows - lat_shift
    row_valid = (row_global >= 0) & (row_global < WIN_LAT * lax.axis_size("lat"))
    own_rows = jnp.arange(WIN_LAT, dtype=jnp.int32)
    row_match = (
        (own_rows[:, None] + lat_shift) // WIN_LAT == region_rows[None, :] // WIN_LAT
    ) & row_valid[None, :]
    region_cols = jnp.arange(cols_dev + WIN_LON, dtype=jnp.int32)
    own_cols = jnp.arange(cols_dev, dtype=jnp.int32)
    col_match = (own_cols[:, None] + lon_shift) // WIN_LON == region_cols[None, :] // WIN_LON
    cell_match = row_match[None, :, None, None, :, None] & col_match[None, None, :, None, None, :]
    key_mask = jnp.broadcast_to(
        cell_match, (levels_dev, WIN_LAT, cols_dev, levels_dev, 2 * WIN_LAT, cols_dev + WIN_LON)
    ).reshape(query_own.shape[0], key_region.shape[0])
    scores = jnp.einsum(
        "qhd,khd->hqk", query_own, key_region, preferred_element_type=jnp.float32
    ) * HEAD_DIM ** (-0.5)
    scores = jnp.where(key_mask[None], scores, -1e30)
    shifted = scores - jnp.max(scores, axis=-1, keepdims=True)
    weights = jnp.exp(shifted)
    probs = (weights / jnp.sum(weights, axis=-1, keepdims=True)).astype(jnp.bfloat16)
    attended = jnp.einsum(
        "hqk,khd->qhd", probs, value_region, preferred_element_type=jnp.float32
    ).reshape(-1, width)
    mid = tokens.reshape(-1, width).astype(jnp.float32) + attended
    mean_square = jnp.mean(mid * mid, axis=-1, keepdims=True)
    normed = (mid * lax.rsqrt(mean_square + 1e-06) * norm_gain).astype(jnp.bfloat16)
    logits = jnp.dot(normed, w_router, preferred_element_type=jnp.float32)
    experts_all = w_router.shape[1]
    cell_count = mid.shape[0]
    capacity = min(cell_count, 8 * cell_count // (3 * experts_all))
    chosen = routes.reshape(cell_count, 2)
    expert_ids = jnp.arange(experts_all, dtype=jnp.int32)
    onehot = (chosen[:, :, None] == expert_ids[None, None, :]).astype(jnp.int32)
    picked = jnp.sum(jnp.where(onehot > 0, logits[:, None, :], 0.0), axis=2)
    gate_prob = jax.nn.sigmoid(picked)
    combine = gate_prob / jnp.sum(gate_prob, axis=1, keepdims=True)
    flat_hot = onehot.reshape(2 * cell_count, experts_all)
    slot_index = jnp.sum((jnp.cumsum(flat_hot, axis=0) - flat_hot) * flat_hot, axis=1)
    target = chosen.reshape(-1) * capacity + slot_index
    placed = (
        jnp.arange(experts_all * capacity, dtype=jnp.int32)[:, None] == target[None, :]
    ).reshape(experts_all * capacity, cell_count, 2)
    dispatch_map = jnp.any(placed, axis=2).astype(jnp.bfloat16)
    outgoing = jnp.dot(dispatch_map, normed, preferred_element_type=jnp.float32).astype(
        jnp.bfloat16
    )
    outgoing = outgoing.reshape(experts_all, capacity, width)
    combine_map = jnp.sum(jnp.where(placed, combine[None, :, :], 0.0), axis=2)
    exp_dev = w_gate.shape[0]
    lon_count = lax.axis_size("lon")
    incoming = send_out(outgoing).reshape(lon_count, exp_dev, capacity, width)
    gathered = lax.all_gather(incoming, "exp", axis=0, tiled=True)
    hidden = expert_hidden(gathered, w_gate, w_up)
    summed = lax.psum_scatter(
        jnp.einsum("secf,edf->secd", hidden, w_down, preferred_element_type=jnp.float32).astype(
            jnp.bfloat16
        ),
        "exp",
        scatter_dimension=0,
        tiled=True,
    )
    results = summed.reshape(experts_all, capacity, width)
    returned = send_back(results).reshape(experts_all * capacity, width)
    moe = jnp.einsum(
        "st,sd->td", combine_map, returned.astype(jnp.float32), precision=lax.Precision.HIGHEST
    )
    return (mid + moe).astype(jnp.bfloat16).reshape(tokens.shape)


def solution(mesh):
    in_specs = (
        P("exp", "lat", "lon", None),
        P("exp", "lat", "lon", None),
        P("exp", "lat", "lon", None),
        P("exp", "lat", "lon", None),
        P(),
        P(),
        P(),
        P(),
        P("exp", "lat", "lon", None, None),
        P("lon", None, "exp"),
        P("lon", None, "exp"),
        P("lon", None, "exp"),
    )
    out_specs = P("exp", "lat", "lon", None)
    return jax.shard_map(shards, mesh=mesh, in_specs=in_specs, out_specs=out_specs, check_vma=False)
```

profile of v0, /device:TPU:1, one launch (start us, length us, event | category | flops | bytes accessed | tf_op | source)
XLA Modules:
  0.0 380.8 jit_solution(12678550657105450138)
XLA Ops:
  6.5 2.9 maximum_bitcast_fusion
  9.4 4.6 %collective-permute-start = (bf16[2,2,1,6,1,12,1024]{6,1,5,3,0,4,2:T(2,128)(2,1)}, bf16[2,2,1,6,1,12,1024]{6,1,5,3,0,4,2:T(2,128)(2,1)}, u32[]{:S(2)}, u32[]{:S(2)}) collective-permute-start(bf16[2,2,1,6,1,12,1024]{6,1,5,3,0,4,2:T(2,128)(2,1)} %maximum_bitcast_fusion), channel_id=1, source_target_pairs={{0,16},{16,32},{32,48},{48,64},{64,80},{80,96},{96,112},{112,128},... | collective-permute-start | bytes 1769480 | tf_op jit(solution)/shard_map/ppermute | solution.py:18
  14.0 6.1 %collective-permute-start.1 = (bf16[2,2,1,6,1,12,1024]{6,1,5,3,0,4,2:T(2,128)(2,1)}, bf16[2,2,1,6,1,12,1024]{6,1,5,3,0,4,2:T(2,128)(2,1)}, u32[]{:S(2)}, u32[]{:S(2)}) collective-permute-start(bf16[2,2,1,6,1,12,1024]{6,1,5,3,0,4,2:T(2,128)(2,1)} %maximum_bitcast_fusion), channel_id=1, source_target_pairs={{16,0},{32,16},{48,32},{64,48},{80,64},{96,80},{112,96},{128,112},... | collective-permute-start | bytes 1769480 | tf_op jit(solution)/shard_map/ppermute | solution.py:20
  20.1 1.9 copy.59
  22.1 1.8 reshape.307
  23.9 2.0 reshape.305
  27.2 1.8 copy.63
  29.0 2.7 reshape.291
  31.8 5.3 %pad_maximum_fusion.1 = bf16[2,2,1,6,3,12,1024]{6,1,5,3,0,4,2:T(2,128)(2,1)} fusion(bf16[2,2,1,6,1,12,1024]{6,1,5,3,0,4,2:T(2,128)(2,1)} %collective-permute-done.1, bf16[2,2,1,6,1,12,1024]{6,1,5,3,0,4,2:T(2,128)(2,1)} %maximum_bitcast_fusion, bf16[2,2,1,6,1,12,1024]{6,1,5,3,0,4,2:T(2,128)(2,1)} %collective-permute-done), kind=kLoop, calls=%fused_computation.21 | loop fusion | flops 1769472 | bytes 3538944 | tf_op jit(solution)/shard_map/concatenate | solution.py:16
  37.0 2.0 collective-permute-start.2
  39.1 6.9 %collective-permute-start.3 = (bf16[2,2,1,6,3,12,1024]{6,1,5,3,0,4,2:T(2,128)(2,1)}, bf16[2,2,1,6,3,12,1024]{6,1,5,3,0,4,2:T(2,128)(2,1)}, u32[]{:S(2)}, u32[]{:S(2)}) collective-permute-start(bf16[2,2,1,6,3,12,1024]{6,1,5,3,0,4,2:T(2,128)(2,1)} %pad_maximum_fusion.1), channel_id=1, source_target_pairs={{4,0},{8,4},{12,8},{0,12},{5,1},{9,5},{13,9},{1,13},{6,2},{10,6},{... | collective-permute-start | bytes 5308424 | tf_op jit(solution)/shard_map/ppermute | solution.py:20
  47.4 3.0 broadcast_in_dim.37
  50.3 2.2 copy.75
  55.0 25.2 %collective-permute-done.2 = bf16[2,2,1,6,3,12,1024]{6,1,5,3,0,4,2:T(2,128)(2,1)} collective-permute-done((bf16[2,2,1,6,3,12,1024]{6,1,5,3,0,4,2:T(2,128)(2,1)}, bf16[2,2,1,6,3,12,1024]{6,1,5,3,0,4,2:T(2,128)(2,1)}, u32[]{:S(2)}, u32[]{:S(2)}) %collective-permute-start.2) | collective-permute-done | bytes 1769504 | tf_op jit(solution)/shard_map/ppermute | solution.py:18
  80.2 39.1 %collective-permute-done.3 = bf16[2,2,1,6,3,12,1024]{6,1,5,3,0,4,2:T(2,128)(2,1)} collective-permute-done((bf16[2,2,1,6,3,12,1024]{6,1,5,3,0,4,2:T(2,128)(2,1)}, bf16[2,2,1,6,3,12,1024]{6,1,5,3,0,4,2:T(2,128)(2,1)}, u32[]{:S(2)}, u32[]{:S(2)}) %collective-permute-start.3) | collective-permute-done | bytes 1769504 | tf_op jit(solution)/shard_map/ppermute | solution.py:20
  119.3 11.7 %pad_maximum_fusion = bf16[2,2,3,6,3,12,1024]{6,1,5,3,0,4,2:T(2,128)(2,1)S(1)} fusion(bf16[2,2,1,6,3,12,1024]{6,1,5,3,0,4,2:T(2,128)(2,1)} %collective-permute-done.3, bf16[2,2,1,6,1,12,1024]{6,1,5,3,0,4,2:T(2,128)(2,1)} %collective-permute-done.1, bf16[2,2,1,6,1,12,1024]{6,1,5,3,0,4,2:T(2,128)(2,1)} %maximum_bitcast_fusion, ...), kind=kLoop, calls=%fused_computation.9 | loop fusion | flops 10616832 | bytes 10616832 | tf_op jit(solution)/shard_map/concatenate | solution.py:16
  131.0 5.9 %copy.60 = bf16[2,2,3,6,3,12,1024]{6,1,5,4,3,2,0:T(2,128)(2,1)S(1)} copy(bf16[2,2,3,6,3,12,1024]{6,1,5,3,0,4,2:T(2,128)(2,1)S(1)} %pad_maximum_fusion) | data formatting | bytes 10616832 | tf_op jit(solution)/shard_map/concatenate | solution.py:16
  136.9 2.0 constant_dynamic-slice_fusion
  139.2 4.7 %reshape_squeeze.7 = bf16[576,32,32]{2,1,0:T(8,128)(2,1)} reshape(bf16[1,2,12,24,1024]{4,3,2,1,0:T(8,128)(2,1)S(1)} %copy.62) | data formatting | bytes 2359296 | tf_op jit(solution)/shard_map/reshape;squeeze | solution.py:71
  144.3 5.0 %reshape_squeeze.6 = bf16[576,32,32]{2,1,0:T(8,128)(2,1)} reshape(bf16[1,2,12,24,1024]{4,3,2,1,0:T(8,128)(2,1)S(1)} %copy.61) | data formatting | bytes 2359296 | tf_op jit(solution)/shard_map/reshape;squeeze | solution.py:72
  149.3 13.0 %fusion.7 = f32[32,576,144]{1,2,0:T(8,128)} fusion(bf16[576,32,32]{2,1,0:T(8,128)(2,1)} %reshape_squeeze.7, bf16[144,32,32]{2,1,0:T(8,128)(2,1)S(1)} %copy-done.1), kind=kOutput, calls=%fused_computation.11 | convolution fusion | flops 169869312 | bytes 12091392 | tf_op jit(solution)/shard_map/qhd,khd->hqk/dot_general | solution.py:88
  162.3 17.3 %fusion.30 = (f32[32,144]{1,0:T(8,128)S(1)}, f32[32,144,576]{2,1,0:T(8,128)}) fusion(f32[32,576,144]{1,2,0:T(8,128)} %fusion.7, pred[144,576]{1,0:T(8,128)(4,1)S(1)} %copy-done.4), kind=kOutput, calls=%fused_computation.77 | output fusion | flops 15925823 | bytes 21335040 | tf_op jit(solution)/shard_map/sub | solution.py:92
  179.7 10.0 %fusion.22 = (f32[144]{0:T(256)S(1)}, f32[32,32,144]{2,1,0:T(8,128)}) fusion(f32[144,32,32]{0,2,1:T(8,128)} %copy.75, f32[32,144,576]{2,1,0:T(8,128)} %get-tuple-element.8, f32[32,144]{1,0:T(8,128)S(1)} %get-tuple-element.7, bf16[576,32,32]{2,1,0:T(8,128)(2,1)S(1)} %bitcast.118), kind=kOutput, calls=%fused_computation.33 | convolution fusion | flops 175619952 | bytes 12995136 | tf_op jit(solution)/shard_map/hqk,khd->qhd/dot_general | solution.py:95
  192.5 38.2 %all_to_all.10 = bf16[32,12,1024]{2,1,0:T(8,128)(2,1)S(1)} all-to-all(bf16[32,12,1024]{2,1,0:T(8,128)(2,1)S(1)} %reshape.295), channel_id=1, replica_groups=mesh['lon'=32,'lat'=4,'exp'=4] {'lon'}, dimensions={0} | all-to-all | bytes 1572864 | tf_op jit(solution)/shard_map/all_to_all | solution.py:34
  232.1 43.1 %all-gather.3.cloned.1.call-done = bf16[128,12,1024]{2,0,1:T(8,128)(2,1)} async-done(((bf16[32,12,1024]{2,0,1:T(8,128)(2,1)}), bf16[128,12,1024]{2,0,1:T(8,128)(2,1)}) %all-gather.3.cloned.1.call-update) | async-done | bytes 3145744 | tf_op jit(solution)/shard_map/all_gather | solution.py:126
  275.2 5.7 %fusion.19 = f32[128,12,512]{2,0,1:T(8,128)} fusion(bf16[128,12,1024]{2,0,1:T(8,128)(2,1)} %all-gather.3.cloned.1.call-done, bf16[1,1024,512]{2,1,0:T(8,128)(2,1)} %param.21), kind=kOutput, calls=%fused_computation.29 | convolution fusion | flops 1610612736 | bytes 7340032 | tf_op jit(solution)/shard_map/secd,edf->secf/dot_general | solution.py:28
  280.8 8.3 %convert_bitcast_fusion = bf16[128,1,12,1024]{3,0,2,1:T(8,128)(2,1)} fusion(f32[128,12,512]{2,0,1:T(8,128)} %fusion.19, bf16[128,12,1024]{2,0,1:T(8,128)(2,1)} %all-gather.3.cloned.1.call-done, bf16[1,1024,512]{2,1,0:T(8,128)(2,1)S(1)} %copy-done, bf16[1,1024,512]{2,1,0:T(8,128)(2,1)S(1)} %copy-done.10), kind=kOutput, calls=%fused_computation.20 | convolution fusion | flops 3227516928 | bytes 11534336 | tf_op jit(solution)/shard_map/secf,edf->secd/dot_general | solution.py:129
  289.1 44.1 %reduce-scatter.2.cloned.1.call-done = bf16[32,1,12,1024]{3,0,2,1:T(8,128)(2,1)} async-done(((bf16[128,1,12,1024]{3,0,2,1:T(8,128)(2,1)}), bf16[32,1,12,1024]{3,0,2,1:T(8,128)(2,1)}) %reduce-scatter.2.cloned.1.call-update) | async-done | bytes 786448 | tf_op jit(solution)/shard_map/reduce_scatter | solution.py:128
  333.2 2.6 copy.77
  335.8 8.6 %all-to-all-start.1 = ((bf16[32,12,1024]{2,1,0:T(8,128)(2,1)}), bf16[32,12,1024]{2,1,0:T(8,128)(2,1)S(1)}, u32[]{:S(2)}, u32[]{:S(2)}) async-start(bf16[32,12,1024]{2,1,0:T(8,128)(2,1)} %copy.77), calls=%async_computation.2 | async-start | bytes 2097152 | tf_op jit(solution)/shard_map/all_to_all | solution.py:38
  345.7 25.2 %all-to-all-done.1 = bf16[32,12,1024]{2,1,0:T(8,128)(2,1)S(1)} async-done(((bf16[32,12,1024]{2,1,0:T(8,128)(2,1)}), bf16[32,12,1024]{2,1,0:T(8,128)(2,1)S(1)}, u32[]{:S(2)}, u32[]{:S(2)}) %all-to-all-start.1) | async-done | bytes 786464 | tf_op jit(solution)/shard_map/all_to_all | solution.py:38
  371.0 1.6 fusion.14
  (71 shorter events, 11.2 us)
Async XLA Ops:
  6.5 274.3 %copy-start = (bf16[1,1024,512]{2,1,0:T(8,128)(2,1)S(1)}, bf16[1,1024,512]{2,1,0:T(8,128)(2,1)}, u32[]{:S(2)}) copy-start(bf16[1,1024,512]{2,1,0:T(8,128)(2,1)} %param.23) | copy-start | bytes 3145732
  6.5 268.6 %all-gather.3.cloned.1.call-start = ((), (), s32[]{:S(2)}) async-start(), calls=%async_computation.4 | async-start | bytes 3932160 | tf_op jit(solution)/shard_map/all_gather | solution.py:126
  9.4 22.4 %collective-permute-start = (bf16[2,2,1,6,1,12,1024]{6,1,5,3,0,4,2:T(2,128)(2,1)}, bf16[2,2,1,6,1,12,1024]{6,1,5,3,0,4,2:T(2,128)(2,1)}, u32[]{:S(2)}, u32[]{:S(2)}) collective-permute-start(bf16[2,2,1,6,1,12,1024]{6,1,5,3,0,4,2:T(2,128)(2,1)} %maximum_bitcast_fusion), channel_id=1, source_target_pairs={{0,16},{16,32},{32,48},{48,64},{64,80},{80,96},{96,112},{112,128},... | collective-permute-start | bytes 1769480 | tf_op jit(solution)/shard_map/ppermute | solution.py:18
  14.0 17.8 %collective-permute-start.1 = (bf16[2,2,1,6,1,12,1024]{6,1,5,3,0,4,2:T(2,128)(2,1)}, bf16[2,2,1,6,1,12,1024]{6,1,5,3,0,4,2:T(2,128)(2,1)}, u32[]{:S(2)}, u32[]{:S(2)}) collective-permute-start(bf16[2,2,1,6,1,12,1024]{6,1,5,3,0,4,2:T(2,128)(2,1)} %maximum_bitcast_fusion), channel_id=1, source_target_pairs={{16,0},{32,16},{48,32},{64,48},{80,64},{96,80},{112,96},{128,112},... | collective-permute-start | bytes 1769480 | tf_op jit(solution)/shard_map/ppermute | solution.py:20
  37.0 15.5 %copy-start.9 = (s32[1,1,1,144,2]{3,4,2,1,0:T(2,128)S(1)}, s32[1,1,1,144,2]{3,4,2,1,0:T(2,128)}, u32[]{:S(2)}) copy-start(s32[1,1,1,144,2]{3,4,2,1,0:T(2,128)} %param.20) | copy-start | bytes 3460
  37.0 43.2 %collective-permute-start.2 = (bf16[2,2,1,6,3,12,1024]{6,1,5,3,0,4,2:T(2,128)(2,1)}, bf16[2,2,1,6,3,12,1024]{6,1,5,3,0,4,2:T(2,128)(2,1)}, u32[]{:S(2)}, u32[]{:S(2)}) collective-permute-start(bf16[2,2,1,6,3,12,1024]{6,1,5,3,0,4,2:T(2,128)(2,1)} %pad_maximum_fusion.1), channel_id=1, source_target_pairs={{0,4},{4,8},{8,12},{12,0},{1,5},{5,9},{9,13},{13,1},{2,6},{6,10},{... | collective-permute-start | bytes 5308424 | tf_op jit(solution)/shard_map/ppermute | solution.py:18
  39.1 80.2 %collective-permute-start.3 = (bf16[2,2,1,6,3,12,1024]{6,1,5,3,0,4,2:T(2,128)(2,1)}, bf16[2,2,1,6,3,12,1024]{6,1,5,3,0,4,2:T(2,128)(2,1)}, u32[]{:S(2)}, u32[]{:S(2)}) collective-permute-start(bf16[2,2,1,6,3,12,1024]{6,1,5,3,0,4,2:T(2,128)(2,1)} %pad_maximum_fusion.1), channel_id=1, source_target_pairs={{4,0},{8,4},{12,8},{0,12},{5,1},{9,5},{13,9},{1,13},{6,2},{10,6},{... | collective-permute-start | bytes 5308424 | tf_op jit(solution)/shard_map/ppermute | solution.py:20
  144.3 5.0 %copy-start.1 = (bf16[144,32,32]{2,1,0:T(8,128)(2,1)S(1)}, bf16[144,32,32]{2,1,0:T(8,128)(2,1)}, u32[]{:S(2)}) copy-start(bf16[144,32,32]{2,1,0:T(8,128)(2,1)} %reshape.291) | copy-start | bytes 884740
  149.3 13.1 %copy-start.4 = (pred[144,576]{1,0:T(8,128)(4,1)S(1)}, pred[144,576]{1,0:T(8,128)(4,1)}, u32[]{:S(2)}) copy-start(pred[144,576]{1,0:T(8,128)(4,1)} %broadcast_in_dim.37) | copy-start | bytes 248836
  149.3 30.4 %slice-start = ((s8[4718592]{0:T(1024)(128)(4,1)}), s8[524288]{0:T(1024)(128)(4,1)S(1)}, s32[]{:S(2)}) async-start(s8[4718592]{0:T(1024)(128)(4,1)} %bitcast.117), calls=%async_computation.5 | async-start | bytes 1048576
  162.3 17.4 %slice-start.1 = ((s8[4718592]{0:T(1024)(128)(4,1)}), s8[4194304]{0:T(1024)(128)(4,1)S(1)}, s32[]{:S(2)}) async-start(s8[4718592]{0:T(1024)(128)(4,1)} %bitcast.117), calls=%async_computation.6 | async-start | bytes 8388608
  179.7 11.5 %copy-start.2 = (f32[144,1024]{1,0:T(8,128)S(1)}, f32[144,1024]{1,0:T(8,128)}, u32[]{:S(2)}) copy-start(f32[144,1024]{1,0:T(8,128)} %reshape.305) | copy-start | bytes 1769476
  189.7 2.1 copy-start.3
  189.7 2.1 copy-start.6
  191.2 0.6 copy-start.7
  232.0 48.8 %copy-start.10 = (bf16[1,1024,512]{2,1,0:T(8,128)(2,1)S(1)}, bf16[1,1024,512]{2,1,0:T(8,128)(2,1)}, u32[]{:S(2)}) copy-start(bf16[1,1024,512]{2,1,0:T(8,128)(2,1)} %param.22) | copy-start | bytes 3145732
  232.0 101.2 %reduce-scatter.2.cloned.1.call-start = ((), (), s32[]{:S(2)}) async-start(), calls=%async_computation.3 | async-start | bytes 3932160 | tf_op jit(solution)/shard_map/reduce_scatter | solution.py:128
  289.1 55.3 %copy-start.5 = (bf16[1024,32]{0,1:T(8,128)(2,1)S(1)}, bf16[1024,32]{0,1:T(8,128)(2,1)}, u32[]{:S(2)}) copy-start(bf16[1024,32]{0,1:T(8,128)(2,1)} %param.19) | copy-start | bytes 196612
  289.1 55.3 %copy-start.8 = (f32[144]{0:T(256)S(1)}, f32[144]{0:T(256)}, u32[]{:S(2)}) copy-start(f32[144]{0:T(256)} %copy-done.7) | copy-start | bytes 1732
  335.8 35.1 %all-to-all-start.1 = ((bf16[32,12,1024]{2,1,0:T(8,128)(2,1)}), bf16[32,12,1024]{2,1,0:T(8,128)(2,1)S(1)}, u32[]{:S(2)}, u32[]{:S(2)}) async-start(bf16[32,12,1024]{2,1,0:T(8,128)(2,1)} %copy.77), calls=%async_computation.2 | async-start | bytes 2097152 | tf_op jit(solution)/shard_map/all_to_all | solution.py:38
Sparse Core Ops, SparseCore 0:
  232.1 42.9 all-gather.2
  289.3 43.8 reduce-scatter.1
where the time goes:
time: 387 us; the launch traced here: 381 us
  waiting for transfers between devices  177 us (46%)
  local copies, waits for them, and re-layouts  42.8 us (11%)
  other arithmetic  40.3 us (10%)
  matrix products  39.3 us (10%)
  blocking collectives  38.2 us (10%)
  starting transfers between devices  28.3 us (7%)
  between operations  15.3 us (4%)
    reduce_scatter x1, waiting for transfers between devices, shards(): lax.psum_scatter(jnp.einsum('secf,edf->secd', hidden, w_down, preferred_e...  44.1 us
    all_gather x1, waiting for transfers between devices, shards(): gathered = lax.all_gather(incoming, 'exp', axis=0, tiled=True)  43.1 us
    ppermute x2, waiting for transfers between devices, with_halo(): lax.ppermute(head, axis, [((i + 1) % count, i) for i in range(count)])  39.1 us
    all_to_all x1, blocking collectives, send_out(): lax.all_to_all(outgoing, 'lon', split_axis=0, concat_axis=0, tiled=True)  38.2 us
    all_to_all x1, waiting for transfers between devices, send_back(): lax.all_to_all(results, 'lon', split_axis=0, concat_axis=0, tiled=True)  25.2 us
    ppermute x2, waiting for transfers between devices, with_halo(): lax.ppermute(tail, axis, [(i, (i + 1) % count) for i in range(count)])  25.2 us
    sub x1, other arithmetic, shards(): shifted = scores - jnp.max(scores, axis=-1, keepdims=True)  17.3 us
    concatenate x2, other arithmetic, with_halo(): jnp.concatenate([lax.ppermute(tail, axis, [(i, (i + 1) % count) for i in...  17 us
  transfers between devices with their start and end apart: 7, of which 5 were waited for; matrix products, arithmetic and copies ran while one was open for 5% of the time, Pallas kernels for 0%

commit v1 on v0

v1 whole, which is shorter than its diff:
```python
import jax
import jax.numpy as jnp
from jax import lax
from jax.experimental import pallas as pl
from jax.experimental.pallas import tpu as pltpu
from jax.sharding import PartitionSpec as P

MESH = pl.DeviceIdType.MESH
F32 = jnp.float32
BF16 = jnp.bfloat16

CELLS = 144
PADDED = 192
D = 1024
FB = 256
NF = D // FB
HEAD_DIM = 32
HEADS_FB = FB // HEAD_DIM
N_LON, N_LAT, N_EXP = 32, 4, 4
EXPERTS = 32
CAP = 12
GROUPS = 8
GROUP_ROWS = 4 * CAP
ORDER = ((0, 0), (1, 0), (0, 1), (0, 3), (1, 1), (1, 3), (0, 2), (1, 2))


def iota(shape, dim):
    return lax.broadcasted_iota(jnp.int32, shape, dim)


def div12(n):
    return (n * 43691) >> 19


def div24(n):
    return (n * 43691) >> 20


def hot(mask, dtype=BF16):
    return jnp.where(mask, 1.0, 0.0).astype(dtype)


def dot(a, b):
    return jnp.dot(a, b, preferred_element_type=F32)


def dot_nt(a, b):
    return lax.dot_general(a, b, (((1,), (1,)), ((), ())), preferred_element_type=F32)


def layer_kernel(
    slat, slon, tok, qry, key, val, gain, wr, routes, wg_hbm, wu_hbm, wd_hbm, out,
    wg, wu, wd, pad, kv_own, kv_up, kv_dn, tt, kv_l, kv_r, qx, win, mid, nrm,
    m_row, m_col, q_row, q_col, bias, swap, pick0, pick1, disp, hot0, hot1,
    sbuf, rbuf, z, pr, rlb, rab, bbuf, ybuf, comb,
    w_sem, lat_s, lat_r, lon_s, lon_r, a2a_s, a2a_r, ag_s, ag_r, fw_s, fw_r,
    rl_s, rl_r, ra_s, ra_r, bk_s, bk_r,
):
    me = lax.axis_index("lon")
    lat = lax.axis_index("lat")
    ex = lax.axis_index("exp")
    right, left = lax.rem(ex + 1, N_EXP), lax.rem(ex + N_EXP - 1, N_EXP)

    weights = [
        pltpu.make_async_copy(h, v, w_sem.at[n])
        for n, (h, v) in enumerate(((wg_hbm, wg), (wu_hbm, wu), (wd_hbm, wd)))
    ]
    for copy in weights:
        copy.start()

    barrier = pltpu.get_barrier_semaphore()

    @pl.loop(1, N_LON)
    def _(o):
        pl.semaphore_signal(
            barrier, inc=1, device_id={"lon": lax.rem(me + o, N_LON)}, device_id_type=MESH
        )

    for axis, at, count in (("lat", lat, N_LAT), ("exp", ex, N_EXP)):
        for o in (1, count - 1):
            pl.semaphore_signal(
                barrier, inc=1, device_id={axis: lax.rem(at + o, count)}, device_id_type=MESH
            )

    def remote(src, dst, send, recv, **where):
        return pltpu.make_async_remote_copy(
            src_ref=src, dst_ref=dst, send_sem=send, recv_sem=recv,
            device_id=where, device_id_type=MESH,
        )

    def lat_copy(way, a, f):
        rows, dst, to = (
            (pl.ds(16, 128), kv_up, lax.rem(lat + 1, N_LAT)),
            (pl.ds(0, 128), kv_dn, lax.rem(lat + N_LAT - 1, N_LAT)),
        )[way]
        return remote(
            kv_own.at[a, f, rows], dst.at[a, f, rows],
            lat_s.at[way, a, f], lat_r.at[way, a, f], lat=to,
        )

    def lon_copy(way, a, f):
        dst, to = ((kv_l, lax.rem(me + 1, N_LON)), (kv_r, lax.rem(me + N_LON - 1, N_LON)))[way]
        return remote(
            tt.at[a, f], dst.at[a, f], lon_s.at[way, a, f], lon_r.at[way, a, f], lon=to
        )

    pad[...] = jnp.zeros_like(pad)

    def dense(ref, natural):
        for i in range(12):
            pad[16 * i : 16 * i + 12, :] = ref[i]
        n, at = iota((CELLS, PADDED), 0), iota((CELLS, PADDED), 1)
        if natural:
            run = div12(n)
            source = 16 * run + (n - 12 * run)
        else:
            row = div24(n)
            rest = n - 24 * row
            lev = div12(rest)
            source = (lev * 6 + row) * 16 + (rest - 12 * lev)
        return dot(hot(source == at), pad[...])

    for a, ref in enumerate((key, val)):
        cells = dense(ref, False).astype(BF16)
        for f in range(NF):
            kv_own[a, f] = cells[:, f * FB : (f + 1) * FB]

    pl.semaphore_wait(barrier, N_LON - 1 + 4)
    for f in range(NF):
        for a in range(2):
            for way in range(2):
                lat_copy(way, a, f).start()

    cells = dense(qry, True)
    head_of = iota((CELLS, FB), 1) >> 5
    for f in range(NF):
        for h in range(HEADS_FB):
            qx[f, h * CELLS : (h + 1) * CELLS] = jnp.where(
                head_of == h, cells[:, f * FB : (f + 1) * FB], 0.0
            ).astype(BF16)
    cells = dense(tok, True)
    for f in range(NF):
        mid[f] = cells[:, f * FB : (f + 1) * FB]

    s, t = slat[0], slon[0]
    n = iota((CELLS, FB), 0)
    m_row[...] = hot(div24(n) < 6 - s, F32)
    m_col[...] = hot(n - 12 * div12(n) < 12 - t, F32)
    run = div12(n)
    q_row[...] = hot(run - 6 * (div12(run * 2)) < 6 - s, F32)
    q_col[...] = hot(n - 12 * run < 12 - t, F32)
    krow = div24(iota((CELLS, CELLS), 1))
    low = jnp.where(krow < 6 - s + 100 * lat, 0.0, -1e30)
    high = jnp.where(krow >= 6 - s - 100 * (N_LAT - 1 - lat), 0.0, -1e30)
    bias[...] = jnp.where(q_row[:, :CELLS] > 0.5, low, high)

    tri = hot(iota((CELLS, CELLS), 0) > iota((CELLS, CELLS), 1))
    eye = iota((CELLS, CELLS), 0) == iota((CELLS, CELLS), 1)
    e = iota((CELLS, EXPERTS), 1)
    before = jnp.zeros((1, EXPERTS), F32)
    spread = jnp.zeros((EXPERTS * CAP, CELLS), F32)
    for k, (one, pick) in enumerate(((hot0, pick0), (hot1, pick1))):
        chosen = jnp.broadcast_to(routes[:, k : k + 1], (CELLS, EXPERTS))
        oh = hot(chosen == e, F32)
        one[...] = oh
        slot = jnp.sum((dot(tri, oh.astype(BF16)) + before) * oh, axis=1, keepdims=True)
        before = before + jnp.sum(oh, axis=0, keepdims=True)
        pos = slot + CAP * jnp.sum(oh * e.astype(F32), axis=1, keepdims=True)
        pick[...] = hot(
            jnp.broadcast_to(pos, (CELLS, EXPERTS * CAP))
            == iota((CELLS, EXPERTS * CAP), 1).astype(F32)
        )
        pos_row = jnp.sum(
            jnp.where(eye, jnp.broadcast_to(pos, (CELLS, CELLS)), 0.0), axis=0, keepdims=True
        )
        spread = spread + hot(
            jnp.broadcast_to(pos_row, (EXPERTS * CAP, CELLS))
            == iota((EXPERTS * CAP, CELLS), 0).astype(F32),
            F32,
        )
    disp[...] = spread.astype(BF16)
    n, at = iota((PADDED, PADDED), 0), iota((PADDED, PADDED), 1)
    outer = div24(n) >> 1
    rest = n - 48 * outer
    inner = div12(rest)
    swap[...] = hot(48 * inner + 12 * outer + (rest - 12 * inner) == at)

    def own_rows(f):
        for a in range(2):
            for way in range(2):
                lat_copy(way, a, f).wait_recv()
            own, up, dn = (r[a, f].astype(F32) for r in (kv_own, kv_up, kv_dn))
            inside = m_row[...] > 0.5
            tt[a, f, 0:CELLS] = jnp.where(inside, own, up).astype(BF16)
            tt[a, f, CELLS : 2 * CELLS] = jnp.where(inside, dn, own).astype(BF16)
            for way in range(2):
                lon_copy(way, a, f).start()

    def attend(f):
        for a in range(2):
            for way in range(2):
                lon_copy(way, a, f).wait_recv()
            inside = m_col[...] > 0.5
            for r in range(2):
                own, lo, hi = (
                    x[a, f, r * CELLS : (r + 1) * CELLS].astype(F32) for x in (tt, kv_l, kv_r)
                )
                win[a, 2 * r] = jnp.where(inside, own, lo).astype(BF16)
                win[a, 2 * r + 1] = jnp.where(inside, hi, own).astype(BF16)
        spread_q = qx[f]
        s_w = [dot_nt(spread_q, win[0, w]) for w in range(4)]
        first_row, first_col = q_row[:, :CELLS] > 0.5, q_col[:, :CELLS] > 0.5
        probs, scale = [], []
        for h in range(HEADS_FB):
            part = [x[h * CELLS : (h + 1) * CELLS] for x in s_w]
            score = jnp.where(
                first_row,
                jnp.where(first_col, part[0], part[1]),
                jnp.where(first_col, part[2], part[3]),
            )
            score = score * HEAD_DIM ** (-0.5) + bias[...]
            weight = jnp.exp(score - jnp.max(score, axis=1, keepdims=True))
            scale.append(1.0 / jnp.sum(weight, axis=1, keepdims=True))
            probs.append(weight.astype(BF16))
        probs = jnp.concatenate(probs, axis=0)
        o_w = [dot(probs, win[1, w]) for w in range(4)]
        first_row, first_col = q_row[...] > 0.5, q_col[...] > 0.5
        total = mid[f]
        for h in range(HEADS_FB):
            part = [x[h * CELLS : (h + 1) * CELLS] for x in o_w]
            got = jnp.where(
                first_row,
                jnp.where(first_col, part[0], part[1]),
                jnp.where(first_col, part[2], part[3]),
            )
            total = total + jnp.where(head_of == h, got * scale[h], 0.0)
        mid[f] = total

    own_rows(0)

    @pl.loop(0, NF)
    def _(f):
        @pl.when(f < NF - 1)
        def _():
            own_rows(f + 1)

        attend(f)

    square = sum(jnp.sum(mid[f] * mid[f], axis=1, keepdims=True) for f in range(NF))
    inv = lax.rsqrt(square * (1.0 / D) + 1e-06)
    for f in range(NF):
        cols = slice(f * FB, (f + 1) * FB)
        nrm[:, cols] = (mid[f] * inv * gain[:, cols]).astype(BF16)
    logits = dot(nrm[...], wr[...])
    gates = [
        jax.nn.sigmoid(jnp.sum(logits * one[...], axis=1, keepdims=True)) for one in (hot0, hot1)
    ]
    for k in range(2):
        comb[k] = jnp.broadcast_to(gates[k] / (gates[0] + gates[1]), (CELLS, 128))

    zl, yp, sm = me // 16, lax.rem(me // 4, 4), lax.rem(me, 4)

    def group(i):
        dz, dy = ORDER[i]
        return lax.rem(zl + dz, 2) * 4 + lax.rem(yp + dy, 4)

    def a2a(d):
        return remote(sbuf.at[d], rbuf.at[me], a2a_s.at[d], a2a_r.at[me], lon=d)

    def a2a_from(d):
        return remote(sbuf.at[d], rbuf.at[d], a2a_s.at[d], a2a_r.at[d], lon=d)

    def back(d):
        return remote(sbuf.at[d], bbuf.at[me], bk_s.at[d], bk_r.at[me], lon=d)

    def back_from(d):
        return remote(sbuf.at[d], bbuf.at[d], bk_s.at[d], bk_r.at[d], lon=d)

    def stacked(rows):
        blocks = jnp.concatenate([rows[:, f * FB : (f + 1) * FB] for f in range(NF)], axis=0)
        return dot(swap[...], blocks).astype(BF16).reshape(4, GROUP_ROWS, FB)

    def unstacked(blocks):
        rows = dot(swap[...], blocks.reshape(PADDED, FB)).astype(BF16)
        return [rows[f * GROUP_ROWS : (f + 1) * GROUP_ROWS] for f in range(NF)]

    for i in range(GROUPS):
        g = group(i)
        routed = dot(disp[pl.ds(pl.multiple_of(g * GROUP_ROWS, 16), GROUP_ROWS)], nrm[...])
        sbuf[pl.ds(g * 4, 4)] = stacked(routed.astype(BF16))
        for o in range(4):
            d = g * 4 + lax.rem(sm + o, 4)
            if i == 0 and o == 0:
                rbuf[d] = sbuf[d]
            else:
                a2a(d).start()

    def ag(way, i):
        return remote(
            z.at[0, i], z.at[1 + way, i], ag_s.at[way, i], ag_r.at[way, i],
            exp=(right, left)[way],
        )

    def fw(i):
        way = i % 2
        return remote(
            z.at[1 + way, i], z.at[3, i], fw_s.at[i], fw_r.at[i], exp=(right, left)[way]
        )

    def forward(i):
        ag(0, i).wait_recv()
        ag(1, i).wait_recv()
        fw(i).start()

    for i in range(GROUPS):
        g = group(i)
        for o in range(4):
            if not (i == 0 and o == 0):
                a2a_from(g * 4 + lax.rem(sm + o, 4)).wait_recv()
        for f, rows in enumerate(unstacked(rbuf[pl.ds(g * 4, 4)])):
            z[0, i, :, f * FB : (f + 1) * FB] = rows
        ag(0, i).start()
        ag(1, i).start()
        if i >= 2:
            forward(i - 2)

    for copy in weights:
        copy.wait()

    def ffn(plane, half):
        rows = z[plane, 4 * half : 4 * half + 4].reshape(PADDED, D)
        gate = dot(rows, wg[...])
        up = dot(rows, wu[...])
        hidden = (gate / (1.0 + jnp.exp(-gate)) * up).astype(BF16)
        down = dot_nt(hidden, wd[...]).astype(BF16)
        pr[plane, 4 * half : 4 * half + 4] = down.reshape(4, GROUP_ROWS, D)

    def rl(i):
        return remote(
            pr.at[3, i], rlb.at[i], rl_s.at[i], rl_r.at[i], exp=(right, left)[i % 2]
        )

    def ra(way, i):
        return remote(
            pr.at[2 - way, i], rab.at[way, i], ra_s.at[way, i], ra_r.at[way, i],
            exp=(right, left)[way],
        )

    def halves(half):
        return range(4 * half, 4 * half + 4)

    def direct(half):
        for i in halves(half):
            ra(1 - i % 2, i).start()

    def relay(half):
        for i in halves(half):
            fw(i).wait_recv()
        ffn(3, half)
        for i in halves(half):
            rl(i).start()

    def relayed(half):
        for i in halves(half):
            way = i % 2
            rl(i).wait_recv()
            pr[2 - way, i] = (pr[2 - way, i].astype(F32) + rlb[i].astype(F32)).astype(BF16)
            ra(way, i).start()

    def finish(half):
        for i in halves(half):
            ra(0, i).wait_recv()
            ra(1, i).wait_recv()
            rows = pr[0, i].astype(F32) + rab[0, i].astype(F32) + rab[1, i].astype(F32)
            blocks = stacked(rows.astype(BF16))
            g = group(i)
            if i == 0:
                for o in range(1, 4):
                    a2a(g * 4 + lax.rem(sm + o, 4)).wait_send()
            else:
                for o in range(4):
                    a2a(g * 4 + lax.rem(sm + o, 4)).wait_send()
            sbuf[pl.ds(g * 4, 4)] = blocks
            for o in range(4):
                d = g * 4 + lax.rem(sm + o, 4)
                if i == 0 and o == 0:
                    bbuf[d] = sbuf[d]
                else:
                    back(d).start()

    ffn(0, 0)
    forward(6)
    ffn(1, 0)
    ffn(2, 0)
    direct(0)
    forward(7)
    relay(0)
    ffn(0, 1)
    ffn(1, 1)
    ffn(2, 1)
    relayed(0)
    direct(1)
    relay(1)
    finish(0)
    relayed(1)
    finish(1)

    for i in range(GROUPS):
        g = group(i)
        for o in range(4):
            if not (i == 0 and o == 0):
                back_from(g * 4 + lax.rem(sm + o, 4)).wait_recv()
        at = pl.ds(pl.multiple_of(g * GROUP_ROWS, 16), GROUP_ROWS)
        for f, rows in enumerate(unstacked(bbuf[pl.ds(g * 4, 4)])):
            ybuf[at, f * FB : (f + 1) * FB] = rows
    n, at = iota((PADDED, CELLS), 0), iota((PADDED, CELLS), 1)
    run, col = n >> 4, n & 15
    widen = hot((run * 12 + col == at) & (col < 12))
    for f in range(NF):
        cols = slice(f * FB, (f + 1) * FB)
        moe = comb[0, :, :1] * dot(pick0[...], ybuf[:, cols])
        moe = moe + comb[1, :, :1] * dot(pick1[...], ybuf[:, cols])
        full = dot(widen, (mid[f] + moe).astype(BF16)).astype(BF16)
        for i in range(12):
            out[i, :, cols] = full[16 * i : 16 * i + 12]

    @pl.loop(0, NF)
    def _(f):
        for a in range(2):
            for way in range(2):
                lat_copy(way, a, f).wait_send()
                lon_copy(way, a, f).wait_send()

    for i in range(GROUPS):
        fw(i).wait_send()
        rl(i).wait_send()
        for way in range(2):
            ag(way, i).wait_send()
            ra(way, i).wait_send()

    @pl.loop(1, N_LON)
    def _(o):
        back(lax.rem(me + o, N_LON)).wait_send()


def shards(
    tokens, queries, keys, values, shift_lat, shift_lon, norm_gain, w_router, routes,
    w_gate, w_up, w_down,
):
    def flat(x):
        return x.reshape(12, 12, D)

    smem = pl.BlockSpec(memory_space=pltpu.SMEM)
    vmem = pl.BlockSpec(memory_space=pltpu.VMEM)
    hbm = pl.BlockSpec(memory_space=pl.ANY)
    dma = pltpu.SemaphoreType.DMA
    kv = pltpu.VMEM((2, NF, CELLS, FB), BF16)
    kv2 = pltpu.VMEM((2, NF, 2 * CELLS, FB), BF16)
    blocks = pltpu.VMEM((N_LON, GROUP_ROWS, FB), BF16)
    planes = pltpu.VMEM((N_EXP, GROUPS, GROUP_ROWS, D), BF16)
    mask = pltpu.VMEM((CELLS, FB), F32)
    ff = w_gate.shape[2]
    out = pl.pallas_call(
        layer_kernel,
        out_shape=jax.ShapeDtypeStruct((12, 12, D), BF16),
        in_specs=[smem] * 2 + [vmem] * 7 + [hbm] * 3,
        out_specs=vmem,
        scratch_shapes=[
            pltpu.VMEM((D, ff), BF16), pltpu.VMEM((D, ff), BF16), pltpu.VMEM((D, ff), BF16),
            pltpu.VMEM((PADDED, D), BF16),
            kv, kv, kv, kv2, kv2, kv2,
            pltpu.VMEM((NF, HEADS_FB * CELLS, FB), BF16),
            pltpu.VMEM((2, 4, CELLS, FB), BF16),
            pltpu.VMEM((NF, CELLS, FB), F32),
            pltpu.VMEM((CELLS, D), BF16),
            mask, mask, mask, mask,
            pltpu.VMEM((CELLS, CELLS), F32),
            pltpu.VMEM((PADDED, PADDED), BF16),
            pltpu.VMEM((CELLS, EXPERTS * CAP), BF16), pltpu.VMEM((CELLS, EXPERTS * CAP), BF16),
            pltpu.VMEM((EXPERTS * CAP, CELLS), BF16),
            pltpu.VMEM((CELLS, EXPERTS), F32), pltpu.VMEM((CELLS, EXPERTS), F32),
            blocks, blocks,
            planes, planes,
            pltpu.VMEM((GROUPS, GROUP_ROWS, D), BF16),
            pltpu.VMEM((2, GROUPS, GROUP_ROWS, D), BF16),
            blocks,
            pltpu.VMEM((EXPERTS * CAP, D), BF16),
            pltpu.VMEM((2, CELLS, 128), F32),
            dma((3,)),
            dma((2, 2, NF)), dma((2, 2, NF)), dma((2, 2, NF)), dma((2, 2, NF)),
            dma((N_LON,)), dma((N_LON,)),
            dma((2, GROUPS)), dma((2, GROUPS)), dma((GROUPS,)), dma((GROUPS,)),
            dma((GROUPS,)), dma((GROUPS,)), dma((2, GROUPS)), dma((2, GROUPS)),
            dma((N_LON,)), dma((N_LON,)),
        ],
        compiler_params=pltpu.CompilerParams(
            collective_id=0, has_side_effects=True, vmem_limit_bytes=56 * 1024 * 1024
        ),
        cost_estimate=pl.CostEstimate(
            flops=6_000_000_000, bytes_accessed=8_000_000, transcendentals=2_000_000
        ),
    )(
        shift_lat, shift_lon, flat(tokens), flat(queries), flat(keys), flat(values),
        norm_gain.reshape(1, D), w_router, routes.reshape(CELLS, 2),
        w_gate.reshape(D, ff), w_up.reshape(D, ff), w_down.reshape(D, ff),
    )
    return out.reshape(tokens.shape)


def solution(mesh):
    cells = P("exp", "lat", "lon", None)
    weights = P("lon", None, "exp")
    in_specs = (
        cells, cells, cells, cells, P(), P(), P(), P(),
        P("exp", "lat", "lon", None, None), weights, weights, weights,
    )
    return jax.shard_map(
        shards, mesh=mesh, in_specs=in_specs, out_specs=cells, check_vma=False
    )
```

time: 387 us -> 154 us (0.40); the launches traced: 381 us -> 154 us
  waiting for transfers between devices: 177 us -> 0 us
  Pallas kernels: 0 us -> 144 us
  other arithmetic: 40.3 us -> 0 us
  matrix products: 39.3 us -> 0 us
  blocking collectives: 38.2 us -> 0 us
  local copies, waits for them, and re-layouts: 42.8 us -> 7.99 us
  starting transfers between devices: 28.3 us -> 0 us
  between operations: 15.3 us -> 1.36 us
    pallas_call x0 -> x1, Pallas kernels: none -> 144 us  [shards(): pl.pallas_call(layer_kernel, out_shape=jax.ShapeDtypeStruct((12, 12, D),...]
    ppermute x4 -> x0, waiting for transfers between devices: 64.3 us -> none  [the longest x2 39.1 us: with_halo(): lax.ppermute(head, axis, [((i + 1) % count, i) for i in range(count)])]
    reduce_scatter x1 -> x0, waiting for transfers between devices: 44.1 us -> none  [shards(): lax.psum_scatter(jnp.einsum('secf,edf->secd', hidden, w_down, preferred_e...]
    all_gather x1 -> x0, waiting for transfers between devices: 43.1 us -> none  [shards(): gathered = lax.all_gather(incoming, 'exp', axis=0, tiled=True)]
    dot_general x7 -> x0, matrix products: 39.3 us -> none  [the longest x1 13 us: shards(): jnp.einsum('qhd,khd->hqk', query_own, key_region, preferred_element_type=...]
    all_to_all x1 -> x0, blocking collectives: 38.2 us -> none  [send_out(): lax.all_to_all(outgoing, 'lon', split_axis=0, concat_axis=0, tiled=True)]
    all_to_all x1 -> x0, waiting for transfers between devices: 25.2 us -> none  [send_back(): lax.all_to_all(results, 'lon', split_axis=0, concat_axis=0, tiled=True)]
    ppermute x4 -> x0, starting transfers between devices: 19.7 us -> none  [the longest x2 13 us: with_halo(): lax.ppermute(head, axis, [((i + 1) % count, i) for i in range(count)])]
  transfers between devices with their start and end apart: 7 -> 0, of which waited for: 5 -> 0; matrix products, arithmetic and copies ran while one was open for 5% -> 0% of each run, Pallas kernels for 0% -> 0%
where the time goes in v1:
time: 154 us
  Pallas kernels  144 us (94%)
  local copies, waits for them, and re-layouts  7.99 us (5%)
    pallas_call x1, Pallas kernels, shards(): pl.pallas_call(layer_kernel, out_shape=jax.ShapeDtypeStruct((12, 12, D),...  144 us
    unnamed x16, local copies, waits for them, and re-layouts  5.98 us

profile of v1, /device:TPU:1, one launch (start us, length us, event | category | flops | bytes accessed | tf_op | source)
XLA Modules:
  0.0 153.6 jit_solution(7965514487505808610)
XLA Ops:
  0.0 0.0 copy-start.4
  0.0 0.0 copy-start
  1.4 1.4 copy.17
  2.8 0.0 copy-done.4
  2.8 0.8 copy.18.wr
  3.6 0.0 copy-done
  3.6 0.0 copy-start.1
  3.6 0.8 copy.13
  4.4 0.1 copy-done.1
  4.6 0.0 copy-start.2
  4.6 0.8 copy.14
  5.4 0.1 copy-done.2
  5.5 0.0 copy-start.3
  5.5 0.8 copy.15
  6.4 0.1 copy-done.3
  6.5 0.8 copy.16
  7.3 144.3 %shard_map.118 = bf16[12,12,1024]{2,1,0:T(8,128)(2,1)} custom-call(s32[1]{0:T(128)S(6)} %copy.20.slat, s32[1]{0:T(128)S(6)} %copy.21.slon, bf16[12,12,1024]{2,1,0:T(8,128)(2,1)} %bitcast.11, bf16[12,12,1024]{2,1,0:T(8,128)(2,1)} %bitcast.12, bf16[12,12,1024]{2,1,0:T(8,128)(2,1)} %bitcast.13, bf16[12,12,1024]{2,1,0:T(8,128)(2,1)} %bitcast.14, ...), custom_call_target="tpu_custom_call" | custom-call | flops 6000000000 | bytes 8000000 | tf_op jit(solution)/shard_map/pallas_call | solution.py:463
  151.6 2.0 %copy.19 = bf16[2,6,12,1024]{3,0,2,1:T(2,128)(2,1)} copy(bf16[2,6,12,1024]{3,2,1,0:T(8,128)(2,1)} %bitcast.10) | data formatting | bytes 589824 | tf_op jit(solution)/shard_map/reshape | solution.py:507
Async XLA Ops:
  0.0 2.8 %copy-start.4 = (bf16[1024,32]{0,1:T(8,128)(2,1)S(1)}, bf16[1024,32]{0,1:T(8,128)(2,1)}, u32[]{:S(2)}) copy-start(bf16[1024,32]{0,1:T(8,128)(2,1)} %param.19) | copy-start | bytes 196612
  0.0 3.6 %copy-start = (bf16[2,6,12,1024]{3,0,2,1:T(2,128)(2,1)S(1)}, bf16[2,6,12,1024]{3,0,2,1:T(2,128)(2,1)}, u32[]{:S(2)}) copy-start(bf16[2,6,12,1024]{3,0,2,1:T(2,128)(2,1)} %param.12) | copy-start | bytes 884740
  3.6 1.0 copy-start.1
  4.6 1.0 copy-start.2
  5.5 1.0 copy-start.3

commit v2 on v1

v2 whole, which is shorter than its diff:
```python
import functools

import jax
import jax.numpy as jnp
from jax import lax
from jax.experimental import pallas as pl
from jax.experimental.pallas import tpu as pltpu
from jax.sharding import PartitionSpec as P

MESH = pl.DeviceIdType.MESH
F32 = jnp.float32
BF16 = jnp.bfloat16

CELLS = 144
D = 1024
LANES = 128
RUNS = CELLS * D // LANES
FB = 256
NF = D // FB
HEAD_DIM = 32
HEADS_FB = FB // HEAD_DIM
N_LON, N_LAT, N_EXP = 32, 4, 4
EXPERTS = 32
CAP = 12
GROUPS = 8
GROUP_ROWS = 4 * CAP
STACK = 4 * GROUP_ROWS
HALF = 72
SENT = 224
BACK = 80
ORDER = ((0, 0), (1, 0), (0, 1), (0, 3), (1, 1), (1, 3), (0, 2), (1, 2))


def iota(shape, dim):
    return lax.broadcasted_iota(jnp.int32, shape, dim)


def div12(n):
    return (n * 43691) >> 19


def div24(n):
    return (n * 43691) >> 20


def hot(mask, dtype=BF16):
    return jnp.where(mask, 1.0, 0.0).astype(dtype)


def dot(a, b):
    return jnp.dot(a, b, preferred_element_type=F32)


def dot_nt(a, b):
    return lax.dot_general(a, b, (((1,), (1,)), ((), ())), preferred_element_type=F32)


def layer_kernel(
    side, slat, slon, tok, qry, key, val, gain, wr, routes, wg_hbm, wu_hbm, wd_hbm, out,
    wg, wu, wd, qkv, sent, got, kv, kv_up, kv_dn, qx, ret, ret_got, mid, nrm,
    m_low, m_high, m_row, m_in, bias, pick_lon, put_lon, pick_ret, put_ret, untile, swap,
    pick0, pick1, disp, hot0, hot1, sbuf, rbuf, z, pr, rlb, rab, bbuf, ybuf, comb,
    w_sem, lat_s, lat_r, lon_s, lon_r, ret_s, ret_r, a2a_s, a2a_r, ag_s, ag_r, fw_s, fw_r,
    rl_s, rl_r, ra_s, ra_r, bk_s, bk_r,
):
    me = lax.axis_index("lon")
    lat = lax.axis_index("lat")
    ex = lax.axis_index("exp")
    right, left = lax.rem(ex + 1, N_EXP), lax.rem(ex + N_EXP - 1, N_EXP)
    east, west = lax.rem(me + 1, N_LON), lax.rem(me + N_LON - 1, N_LON)
    first = 0 if side else 12

    barrier = pltpu.get_barrier_semaphore()

    @pl.loop(1, N_LON)
    def _(o):
        pl.semaphore_signal(
            barrier, inc=1, device_id={"lon": lax.rem(me + o, N_LON)}, device_id_type=MESH
        )

    for axis, at, count in (("lat", lat, N_LAT), ("exp", ex, N_EXP)):
        for o in (1, count - 1):
            pl.semaphore_signal(
                barrier, inc=1, device_id={axis: lax.rem(at + o, count)}, device_id_type=MESH
            )

    weights = [
        pltpu.make_async_copy(h, v, w_sem.at[n])
        for n, (h, v) in enumerate(((wg_hbm, wg), (wu_hbm, wu), (wd_hbm, wd)))
    ]
    for copy in weights:
        copy.start()

    def remote(src, dst, send, recv, **where):
        return pltpu.make_async_remote_copy(
            src_ref=src, dst_ref=dst, send_sem=send, recv_sem=recv,
            device_id=where, device_id_type=MESH,
        )

    def lon_copy(f):
        return remote(sent.at[f], got.at[f], lon_s.at[f], lon_r.at[f], lon=(east, west)[side])

    def ret_copy(f):
        return remote(ret.at[f], ret_got.at[f], ret_s.at[f], ret_r.at[f], lon=(west, east)[side])

    def lat_copy(way, f):
        rows, dst, to = (
            (pl.ds(16, 128), kv_up, lax.rem(lat + 1, N_LAT)),
            (pl.ds(0, 128), kv_dn, lax.rem(lat + N_LAT - 1, N_LAT)),
        )[way]
        return remote(
            kv.at[f, :, rows], dst.at[f, :, rows], lat_s.at[way, f], lat_r.at[way, f], lat=to
        )

    n, at = iota((LANES, LANES), 0), iota((LANES, LANES), 1)
    untile[...] = hot(((n & 15) >> 1) * 16 + (n >> 4) * 2 + (n & 1) == at)

    def dense(ref, store):
        for b in range(CELLS // 16):
            rows = dot(untile[...], ref[b * LANES : (b + 1) * LANES])
            for j in range(D // LANES):
                f, c = j // 2, (j % 2) * LANES
                store(f, slice(b * 16, b * 16 + 16), slice(c, c + LANES), rows[j * 16 : j * 16 + 16])

    s, t = slat[0], slon[0]
    for a, ref in enumerate((qry, key, val)):

        def to_qkv(f, rows, cols, part, a=a):
            qkv[f, a * CELLS + rows.start : a * CELLS + rows.stop, cols] = part.astype(BF16)

        dense(ref, to_qkv)
    n, at = iota((SENT, 3 * CELLS), 0), iota((SENT, 3 * CELLS), 1)
    a = jnp.where(n >= HALF, 1, 0) + jnp.where(n >= 2 * HALF, 1, 0)
    m = n - HALF * a
    row = div12(m)
    source = a * CELLS + row * 24 + first + (m - 12 * row)
    pick_lon[...] = hot((source == at) & (n < 3 * HALF))
    for f in range(NF):
        sent[f] = dot(pick_lon[...], qkv[f]).astype(BF16)

    pl.semaphore_wait(barrier, N_LON - 1 + 4)
    for f in range(NF):
        lon_copy(f).start()

    n = iota((CELLS, FB), 0)
    row = div24(n)
    rest = n - 24 * row
    at_top, at_bottom = jnp.where(lat == 0, 100, 0), jnp.where(lat == N_LAT - 1, 100, 0)
    m_row[...] = hot(row < 6 - s, F32)
    m_low[...] = hot(row < 6 - s + at_top, F32)
    m_high[...] = hot(row < 6 - s - at_bottom, F32)
    columns = (rest >> 1) < 12 - t
    m_in[...] = hot(columns, F32) if side == 0 else 1.0 - hot(columns, F32)

    shape = (3 * CELLS, 3 * CELLS + SENT)
    n, at = iota(shape, 0), iota(shape, 1)
    a = jnp.where(n >= CELLS, 1, 0) + jnp.where(n >= 2 * CELLS, 1, 0)
    m = n - CELLS * a
    row = div24(m)
    rest = m - 24 * row
    inside = (rest >> 1) < 12 - t if side == 0 else (rest >> 1) >= 12 - t
    put_lon[...] = hot(
        at == jnp.where(inside, n, 3 * CELLS + HALF * a + row * 12 + rest - first)
    )
    head_of = iota((CELLS, FB), 1) >> 5

    def own_columns(f):
        lon_copy(f).wait_recv()
        cells = dot(put_lon[...], jnp.concatenate([qkv[f], got[f]], axis=0))
        kv[f, 0] = cells[CELLS : 2 * CELLS].astype(BF16)
        kv[f, 1] = cells[2 * CELLS :].astype(BF16)

        @pl.when(lat < N_LAT - 1)
        def _():
            lat_copy(0, f).start()

        @pl.when(lat > 0)
        def _():
            lat_copy(1, f).start()

        for h in range(HEADS_FB):
            qx[f, h * CELLS : (h + 1) * CELLS] = jnp.where(
                head_of == h, cells[:CELLS], 0.0
            ).astype(BF16)

    @pl.loop(0, NF)
    def _(f):
        own_columns(f)

    def to_mid(f, rows, cols, part):
        mid[f, rows, cols] = part

    dense(tok, to_mid)

    krow = div24(iota((CELLS, CELLS), 1))
    low = jnp.where(krow < 6 - s + 100 * lat, 0.0, -1e30)
    high = jnp.where(krow >= 6 - s - 100 * (N_LAT - 1 - lat), 0.0, -1e30)
    bias[...] = jnp.where(m_row[:, :CELLS] > 0.5, low, high)

    n, at = iota((BACK, CELLS), 0), iota((BACK, CELLS), 1)
    row = div12(n)
    pick_ret[...] = hot(row * 24 + first + (n - 12 * row) == at)
    n, at = iota((CELLS, BACK), 0), iota((CELLS, BACK), 1)
    row = div24(n)
    rest = n - 24 * row - first
    put_ret[...] = hot((row * 12 + rest == at) & (rest >= 0) & (rest < 12))

    tri = hot(iota((CELLS, CELLS), 0) > iota((CELLS, CELLS), 1))
    n, at = iota((CELLS, CELLS), 0), iota((CELLS, CELLS), 1)
    eye = n == at
    ordered = (n & 1) * HALF + (n >> 1) == at
    e = iota((CELLS, EXPERTS), 1).astype(F32)
    before = jnp.zeros((1, EXPERTS), F32)
    spread = jnp.zeros((EXPERTS * CAP, CELLS), F32)
    for k, (one, pick) in enumerate(((hot0, pick0), (hot1, pick1))):
        named = jnp.broadcast_to(routes[k : k + 1, :].astype(F32), (CELLS, CELLS))
        chosen = jnp.sum(jnp.where(ordered, named, 0.0), axis=1, keepdims=True)
        oh = hot(jnp.broadcast_to(chosen, (CELLS, EXPERTS)) == e, F32)
        one[...] = oh
        slot = jnp.sum((dot(tri, oh.astype(BF16)) + before) * oh, axis=1, keepdims=True)
        before = before + jnp.sum(oh, axis=0, keepdims=True)
        pos = slot + CAP * chosen
        pick[...] = hot(
            jnp.broadcast_to(pos, (CELLS, EXPERTS * CAP))
            == iota((CELLS, EXPERTS * CAP), 1).astype(F32)
        )
        pos_row = jnp.sum(
            jnp.where(eye, jnp.broadcast_to(pos, (CELLS, CELLS)), 0.0), axis=0, keepdims=True
        )
        spread = spread + hot(
            jnp.broadcast_to(pos_row, (EXPERTS * CAP, CELLS))
            == iota((EXPERTS * CAP, CELLS), 0).astype(F32),
            F32,
        )
    disp[...] = spread.astype(BF16)
    n, at = iota((STACK, STACK), 0), iota((STACK, STACK), 1)
    outer = div24(n) >> 1
    rest = n - 48 * outer
    inner = div12(rest)
    swap[...] = hot(48 * inner + 12 * outer + (rest - 12 * inner) == at)

    def attend(f):
        @pl.when(lat > 0)
        def _():
            lat_copy(0, f).wait_recv()

        @pl.when(lat < N_LAT - 1)
        def _():
            lat_copy(1, f).wait_recv()

        win = []
        for a in range(2):
            own, up, dn = (r[f, a].astype(F32) for r in (kv, kv_up, kv_dn))
            win.append(
                (
                    jnp.where(m_low[...] > 0.5, own, up).astype(BF16),
                    jnp.where(m_high[...] > 0.5, dn, own).astype(BF16),
                )
            )
        spread_q = qx[f]
        s_w = [dot_nt(spread_q, w) for w in win[0]]
        first_row = m_row[:, :CELLS] > 0.5
        probs, scale = [], []
        for h in range(HEADS_FB):
            part = [x[h * CELLS : (h + 1) * CELLS] for x in s_w]
            score = jnp.where(first_row, part[0], part[1]) * HEAD_DIM ** (-0.5) + bias[...]
            weight = jnp.exp(score - jnp.max(score, axis=1, keepdims=True))
            scale.append(1.0 / jnp.sum(weight, axis=1, keepdims=True))
            probs.append(weight.astype(BF16))
        probs = jnp.concatenate(probs, axis=0)
        o_w = [dot(probs, w) for w in win[1]]
        first_row = m_row[...] > 0.5
        total = jnp.zeros((CELLS, FB), F32)
        for h in range(HEADS_FB):
            part = [x[h * CELLS : (h + 1) * CELLS] for x in o_w]
            heads = jnp.where(first_row, part[0], part[1]) * scale[h]
            total = jnp.where(head_of == h, heads, total)
        ret[f] = dot(pick_ret[...], total.astype(BF16)).astype(BF16)
        ret_copy(f).start()
        mid[f] = mid[f] + jnp.where(m_in[...] > 0.5, total, 0.0)

    @pl.loop(0, NF)
    def _(f):
        attend(f)

    for f in range(NF):
        ret_copy(f).wait_recv()
        back_home = dot(put_ret[...], ret_got[f])
        mid[f] = mid[f] + jnp.where(m_in[...] > 0.5, 0.0, back_home)

    square = sum(jnp.sum(mid[f] * mid[f], axis=1, keepdims=True) for f in range(NF))
    inv = lax.rsqrt(square * (1.0 / D) + 1e-06)
    for f in range(NF):
        cols = slice(f * FB, (f + 1) * FB)
        nrm[:, cols] = (mid[f] * inv * gain[:, cols]).astype(BF16)
    logits = dot_nt(nrm[...], wr[...])
    gates = [
        jax.nn.sigmoid(jnp.sum(logits * one[...], axis=1, keepdims=True)) for one in (hot0, hot1)
    ]
    for k in range(2):
        comb[k] = jnp.broadcast_to(gates[k] / (gates[0] + gates[1]), (CELLS, 128))

    zl, yp, sm = me // 16, lax.rem(me // 4, 4), lax.rem(me, 4)

    def group(i):
        dz, dy = ORDER[i]
        return lax.rem(zl + dz, 2) * 4 + lax.rem(yp + dy, 4)

    def a2a(d):
        return remote(sbuf.at[d], rbuf.at[me], a2a_s.at[d], a2a_r.at[me], lon=d)

    def a2a_from(d):
        return remote(sbuf.at[d], rbuf.at[d], a2a_s.at[d], a2a_r.at[d], lon=d)

    def back(d):
        return remote(sbuf.at[d], bbuf.at[me], bk_s.at[d], bk_r.at[me], lon=d)

    def back_from(d):
        return remote(sbuf.at[d], bbuf.at[d], bk_s.at[d], bk_r.at[d], lon=d)

    def stacked(rows):
        blocks = jnp.concatenate([rows[:, f * FB : (f + 1) * FB] for f in range(NF)], axis=0)
        return dot(swap[...], blocks).astype(BF16).reshape(4, GROUP_ROWS, FB)

    def unstacked(blocks):
        rows = dot(swap[...], blocks.reshape(STACK, FB)).astype(BF16)
        return [rows[f * GROUP_ROWS : (f + 1) * GROUP_ROWS] for f in range(NF)]

    ybuf[...] = dot(disp[...], nrm[...]).astype(BF16)
    for i in range(GROUPS):
        g = group(i)
        sbuf[pl.ds(g * 4, 4)] = stacked(
            ybuf[pl.ds(pl.multiple_of(g * GROUP_ROWS, 16), GROUP_ROWS)]
        )
    rbuf[me] = sbuf[me]
    for i in range(GROUPS):
        g = group(i)
        for o in range(4):
            if not (i == 0 and o == 0):
                a2a(g * 4 + lax.rem(sm + o, 4)).start()

    def ag(way, i):
        return remote(
            z.at[0, i], z.at[1 + way, i], ag_s.at[way, i], ag_r.at[way, i],
            exp=(right, left)[way],
        )

    def fw(i):
        way = i % 2
        return remote(
            z.at[1 + way, i], z.at[3, i], fw_s.at[i], fw_r.at[i], exp=(right, left)[way]
        )

    def forward(i):
        ag(0, i).wait_recv()
        ag(1, i).wait_recv()
        fw(i).start()

    def ffn(plane, half):
        rows = z[plane, 4 * half : 4 * half + 4].reshape(STACK, D)
        gate = dot(rows, wg[...])
        up = dot(rows, wu[...])
        hidden = (gate / (1.0 + jnp.exp(-gate)) * up).astype(BF16)
        down = dot_nt(hidden, wd[...]).astype(BF16)
        pr[plane, 4 * half : 4 * half + 4] = down.reshape(4, GROUP_ROWS, D)

    def rl(i):
        return remote(
            pr.at[3, i], rlb.at[i], rl_s.at[i], rl_r.at[i], exp=(right, left)[i % 2]
        )

    def ra(way, i):
        return remote(
            pr.at[2 - way, i], rab.at[way, i], ra_s.at[way, i], ra_r.at[way, i],
            exp=(right, left)[way],
        )

    def halves(half):
        return range(4 * half, 4 * half + 4)

    def direct(half):
        for i in halves(half):
            ra(1 - i % 2, i).start()

    def relay(half):
        for i in halves(half):
            fw(i).wait_recv()
        ffn(3, half)
        for i in halves(half):
            rl(i).start()

    def relayed(half):
        for i in halves(half):
            way = i % 2
            rl(i).wait_recv()
            pr[2 - way, i] = (pr[2 - way, i].astype(F32) + rlb[i].astype(F32)).astype(BF16)
            ra(way, i).start()

    def finish(half):
        for i in halves(half):
            ra(0, i).wait_recv()
            ra(1, i).wait_recv()
            rows = pr[0, i].astype(F32) + rab[0, i].astype(F32) + rab[1, i].astype(F32)
            blocks = stacked(rows.astype(BF16))
            g = group(i)
            if i == 0:
                for o in range(1, 4):
                    a2a(g * 4 + lax.rem(sm + o, 4)).wait_send()
            else:
                for o in range(4):
                    a2a(g * 4 + lax.rem(sm + o, 4)).wait_send()
            sbuf[pl.ds(g * 4, 4)] = blocks
            for o in range(4):
                d = g * 4 + lax.rem(sm + o, 4)
                if i == 0 and o == 0:
                    bbuf[d] = sbuf[d]
                else:
                    back(d).start()

    for copy in weights:
        copy.wait()

    for i in range(GROUPS):
        g = group(i)
        for o in range(4):
            if not (i == 0 and o == 0):
                a2a_from(g * 4 + lax.rem(sm + o, 4)).wait_recv()
        for f, rows in enumerate(unstacked(rbuf[pl.ds(g * 4, 4)])):
            z[0, i, :, f * FB : (f + 1) * FB] = rows
        ag(0, i).start()
        ag(1, i).start()
        if i >= 2:
            forward(i - 2)
        if i >= 5:
            ffn(i - 5, 0)
    direct(0)
    forward(6)
    relay(0)
    forward(7)
    relay(1)
    ffn(1, 1)
    ffn(2, 1)
    direct(1)
    relayed(0)
    ffn(0, 1)
    finish(0)
    relayed(1)
    finish(1)

    for i in range(GROUPS):
        g = group(i)
        for o in range(4):
            if not (i == 0 and o == 0):
                back_from(g * 4 + lax.rem(sm + o, 4)).wait_recv()
        at = pl.ds(pl.multiple_of(g * GROUP_ROWS, 16), GROUP_ROWS)
        for f, rows in enumerate(unstacked(bbuf[pl.ds(g * 4, 4)])):
            ybuf[at, f * FB : (f + 1) * FB] = rows
    for f in range(NF):
        cols = slice(f * FB, (f + 1) * FB)
        moe = comb[0, :, :1] * dot(pick0[...], ybuf[:, cols])
        moe = moe + comb[1, :, :1] * dot(pick1[...], ybuf[:, cols])
        out[:, cols] = (mid[f] + moe).astype(BF16)
    for f in range(NF):
        lon_copy(f).wait_send()
        ret_copy(f).wait_send()

    @pl.when(lat < N_LAT - 1)
    def _():
        for f in range(NF):
            lat_copy(0, f).wait_send()

    @pl.when(lat > 0)
    def _():
        for f in range(NF):
            lat_copy(1, f).wait_send()

    for i in range(GROUPS):
        fw(i).wait_send()
        rl(i).wait_send()
        for way in range(2):
            ag(way, i).wait_send()
            ra(way, i).wait_send()

    @pl.loop(1, N_LON)
    def _(o):
        back(lax.rem(me + o, N_LON)).wait_send()


def shards(
    tokens, queries, keys, values, shift_lat, shift_lon, norm_gain, w_router, routes,
    w_gate, w_up, w_down,
):
    def flat(x):
        return x.reshape(2, 6, 12, D // LANES, LANES).transpose(1, 2, 3, 0, 4).reshape(RUNS, LANES)

    smem = pl.BlockSpec(memory_space=pltpu.SMEM)
    vmem = pl.BlockSpec(memory_space=pltpu.VMEM)
    hbm = pl.BlockSpec(memory_space=pl.ANY)
    dma = pltpu.SemaphoreType.DMA
    kv = pltpu.VMEM((NF, 2, CELLS, FB), BF16)
    lon = pltpu.VMEM((NF, SENT, FB), BF16)
    ret = pltpu.VMEM((NF, BACK, FB), BF16)
    blocks = pltpu.VMEM((N_LON, GROUP_ROWS, FB), BF16)
    planes = pltpu.VMEM((N_EXP, GROUPS, GROUP_ROWS, D), BF16)
    mask = pltpu.VMEM((CELLS, FB), F32)
    slots = EXPERTS * CAP
    ff = w_gate.shape[2]
    scratch = [
        pltpu.VMEM((D, ff), BF16), pltpu.VMEM((D, ff), BF16), pltpu.VMEM((D, ff), BF16),
        pltpu.VMEM((NF, 3 * CELLS, FB), BF16),
        lon, lon, kv, kv, kv,
        pltpu.VMEM((NF, HEADS_FB * CELLS, FB), BF16),
        ret, ret,
        pltpu.VMEM((NF, CELLS, FB), F32),
        pltpu.VMEM((CELLS, D), BF16),
        mask, mask, mask, mask,
        pltpu.VMEM((CELLS, CELLS), F32),
        pltpu.VMEM((SENT, 3 * CELLS), BF16), pltpu.VMEM((3 * CELLS, 3 * CELLS + SENT), BF16),
        pltpu.VMEM((BACK, CELLS), BF16), pltpu.VMEM((CELLS, BACK), BF16),
        pltpu.VMEM((LANES, LANES), BF16),
        pltpu.VMEM((STACK, STACK), BF16),
        pltpu.VMEM((CELLS, slots), BF16), pltpu.VMEM((CELLS, slots), BF16),
        pltpu.VMEM((slots, CELLS), BF16),
        pltpu.VMEM((CELLS, EXPERTS), F32), pltpu.VMEM((CELLS, EXPERTS), F32),
        blocks, blocks, planes, planes,
        pltpu.VMEM((GROUPS, GROUP_ROWS, D), BF16),
        pltpu.VMEM((2, GROUPS, GROUP_ROWS, D), BF16),
        blocks,
        pltpu.VMEM((slots, D), BF16),
        pltpu.VMEM((2, CELLS, 128), F32),
        dma((3,)),
        dma((2, NF)), dma((2, NF)), dma((NF,)), dma((NF,)), dma((NF,)), dma((NF,)),
        dma((N_LON,)), dma((N_LON,)),
        dma((2, GROUPS)), dma((2, GROUPS)), dma((GROUPS,)), dma((GROUPS,)),
        dma((GROUPS,)), dma((GROUPS,)), dma((2, GROUPS)), dma((2, GROUPS)),
        dma((N_LON,)), dma((N_LON,)),
    ]

    def call(side):
        return pl.pallas_call(
            functools.partial(layer_kernel, side),
            out_shape=jax.ShapeDtypeStruct((CELLS, D), BF16),
            in_specs=[smem] * 2 + [vmem] * 7 + [hbm] * 3,
            out_specs=vmem,
            scratch_shapes=scratch,
            compiler_params=pltpu.CompilerParams(
                collective_id=side, has_side_effects=True, vmem_limit_bytes=56 * 1024 * 1024
            ),
            cost_estimate=pl.CostEstimate(
                flops=6_000_000_000, bytes_accessed=8_000_000, transcendentals=1_000_000
            ),
            name=("columns_east", "columns_west")[side],
        )

    out = lax.cond(
        shift_lon[0] <= 6, call(0), call(1),
        shift_lat, shift_lon, flat(tokens), flat(queries), flat(keys), flat(values),
        norm_gain.reshape(1, D), w_router.T, routes.reshape(CELLS, 2).T,
        w_gate.reshape(D, ff), w_up.reshape(D, ff), w_down.reshape(D, ff),
    )
    return out.reshape(6, 12, 2, D).transpose(2, 0, 1, 3)


def solution(mesh):
    cells = P("exp", "lat", "lon", None)
    weights = P("lon", None, "exp")
    in_specs = (
        cells, cells, cells, cells, P(), P(), P(), P(),
        P("exp", "lat", "lon", None, None), weights, weights, weights,
    )
    return jax.shard_map(
        shards, mesh=mesh, in_specs=in_specs, out_specs=cells, check_vma=False
    )
```

time: 154 us -> 136 us (0.88); the launches traced: 154 us -> 133 us
  Pallas kernels: 144 us -> 131 us
  local copies, waits for them, and re-layouts: 7.99 us -> 1.51 us
    pallas_call x1, Pallas kernels: 144 us -> 131 us  [shards(): lax.cond(shift_lon[0] <= 6, call(0), call(1), shift_lat, shift_lon, flat(...]
    unnamed x16 -> x4, local copies, waits for them, and re-layouts: 5.98 us -> 0.68 us
where the time goes in v2:
time: 136 us; the launch traced here: 133 us
  Pallas kernels  131 us (96%)
  local copies, waits for them, and re-layouts  1.51 us (1%)
    pallas_call x1, Pallas kernels, shards(): lax.cond(shift_lon[0] <= 6, call(0), call(1), shift_lat, shift_lon, flat(...  131 us

profile of v2, /device:TPU:1, one launch (start us, length us, event | category | flops | bytes accessed | tf_op | source)
XLA Modules:
  0.0 133.5 jit_solution(13706920042173944643)
XLA Ops:
  0.7 0.0 copy-start
  0.7 0.0 copy-start.1
  0.7 0.7 copy-done
  1.3 0.0 copy-done.1
  1.4 131.3 %conditional.1 = (bf16[144,1024]{1,0:T(8,128)(2,1)S(1)}) conditional(s32[]{:T(128)} %bitcast, (s32[1]{0:T(128)}, s32[1]{0:T(128)}, bf16[1152,128]{1,0:T(8,128)(2,1)}, bf16[1152,128]{1,0:T(8,128)(2,1)}, bf16[1152,128]{1,0:T(8,128)(2,1)}, /*index=5*/bf16[1152,128]{1,0:T(8,128)(2,1)}, f32[1,1024]{1,0:T(1,128)S(1)}, bf16[32,1024]{1,0:T(8,128)(2,1)}, ...), branch_computations={%region_0.0_spmd, %region_1.0_spmd} | conditional | flops 6000000000 | bytes 8000008 | solution.py:555
  1.4 130.8 %columns_west.1 = bf16[144,1024]{1,0:T(8,128)(2,1)S(1)} custom-call(s32[1]{0:T(128)} %get-tuple-element.56.slat, s32[1]{0:T(128)} %get-tuple-element.57.slon, bf16[1152,128]{1,0:T(8,128)(2,1)} %get-tuple-element.58.tok, bf16[1152,128]{1,0:T(8,128)(2,1)} %get-tuple-element.59.qry, bf16[1152,128]{1,0:T(8,128)(2,1)} %get-tuple-element.60.key, ...), custom_call_target="tpu_custom_call" | custom-call | flops 6000000000 | bytes 8000000 | tf_op jit(solution)/shard_map/cond/branch_0_fun/columns_west/pallas_call | solution.py:555
  132.7 0.8 reshape.59
Async XLA Ops:
  0.7 0.7 copy-start
  0.7 0.7 copy-start.1

commit v3 on v2

--- a/solution.py
+++ b/solution.py
@@ -57,7 +57,7 @@
 
 def layer_kernel(
     side, slat, slon, tok, qry, key, val, gain, wr, routes, wg_hbm, wu_hbm, wd_hbm, out,
-    wg, wu, wd, qkv, sent, got, kv, kv_up, kv_dn, qx, ret, ret_got, mid, nrm,
+    wg, wu, wd, wd_t, qkv, sent, got, kv, kv_up, kv_dn, qx, ret, ret_got, mid, nrm,
     m_low, m_high, m_row, m_in, bias, pick_lon, put_lon, pick_ret, put_ret, untile, swap,
     pick0, pick1, disp, hot0, hot1, sbuf, rbuf, z, pr, rlb, rab, bbuf, ybuf, comb,
     w_sem, lat_s, lat_r, lon_s, lon_r, ret_s, ret_r, a2a_s, a2a_r, ag_s, ag_r, fw_s, fw_r,
@@ -238,6 +238,10 @@
     rest = n - 48 * outer
     inner = div12(rest)
     swap[...] = hot(48 * inner + 12 * outer + (rest - 12 * inner) == at)
+
+    for copy in weights:
+        copy.wait()
+    wd_t[...] = wd[...].T
 
     def attend(f):
         @pl.when(lat > 0)
@@ -356,13 +360,14 @@
         ag(1, i).wait_recv()
         fw(i).start()
 
-    def ffn(plane, half):
-        rows = z[plane, 4 * half : 4 * half + 4].reshape(STACK, D)
+    def ffn(plane, count, half):
+        planes, part = pl.ds(plane, count), pl.ds(4 * half, 4)
+        rows = z[planes, part].reshape(count * STACK, D)
         gate = dot(rows, wg[...])
         up = dot(rows, wu[...])
         hidden = (gate / (1.0 + jnp.exp(-gate)) * up).astype(BF16)
-        down = dot_nt(hidden, wd[...]).astype(BF16)
-        pr[plane, 4 * half : 4 * half + 4] = down.reshape(4, GROUP_ROWS, D)
+        down = dot(hidden, wd_t[...]).astype(BF16)
+        pr[planes, part] = down.reshape(count, 4, GROUP_ROWS, D)
 
     def rl(i):
         return remote(
@@ -378,23 +383,21 @@
     def halves(half):
         return range(4 * half, 4 * half + 4)
 
-    def direct(half):
-        for i in halves(half):
-            ra(1 - i % 2, i).start()
+    def direct(i):
+        ra(1 - i % 2, i).start()
 
     def relay(half):
         for i in halves(half):
             fw(i).wait_recv()
-        ffn(3, half)
+        ffn(3, 1, half)
         for i in halves(half):
             rl(i).start()
 
-    def relayed(half):
-        for i in halves(half):
-            way = i % 2
-            rl(i).wait_recv()
-            pr[2 - way, i] = (pr[2 - way, i].astype(F32) + rlb[i].astype(F32)).astype(BF16)
-            ra(way, i).start()
+    def relayed(i):
+        way = i % 2
+        rl(i).wait_recv()
+        pr[2 - way, i] = (pr[2 - way, i].astype(F32) + rlb[i].astype(F32)).astype(BF16)
+        ra(way, i).start()
 
     def finish(half):
         for i in halves(half):
@@ -417,9 +420,6 @@
                 else:
                     back(d).start()
 
-    for copy in weights:
-        copy.wait()
-
     for i in range(GROUPS):
         g = group(i)
         for o in range(4):
@@ -431,20 +431,24 @@
         ag(1, i).start()
         if i >= 2:
             forward(i - 2)
-        if i >= 5:
-            ffn(i - 5, 0)
-    direct(0)
+        if i == 5:
+            ffn(0, 1, 0)
+        if i == 6:
+            ffn(1, 2, 0)
+            for k in halves(0):
+                direct(k)
     forward(6)
     relay(0)
     forward(7)
+    for i in halves(0):
+        relayed(i)
     relay(1)
-    ffn(1, 1)
-    ffn(2, 1)
-    direct(1)
-    relayed(0)
-    ffn(0, 1)
+    ffn(1, 2, 1)
+    for i in halves(1):
+        direct(i)
+        relayed(i)
     finish(0)
-    relayed(1)
+    ffn(0, 1, 1)
     finish(1)
 
     for i in range(GROUPS):
@@ -507,6 +511,7 @@
     ff = w_gate.shape[2]
     scratch = [
         pltpu.VMEM((D, ff), BF16), pltpu.VMEM((D, ff), BF16), pltpu.VMEM((D, ff), BF16),
+        pltpu.VMEM((ff, D), BF16),
         pltpu.VMEM((NF, 3 * CELLS, FB), BF16),
         lon, lon, kv, kv, kv,
         pltpu.VMEM((NF, HEADS_FB * CELLS, FB), BF16),

time: 136 us -> 130 us (0.956); the launches traced: 133 us -> 130 us
  Pallas kernels: 131 us -> 128 us
    pallas_call x1, Pallas kernels: 131 us -> 128 us  [shards(): lax.cond(shift_lon[0] <= 6, call(0), call(1), shift_lat, shift_lon, flat(...]
where the time goes in v3:
time: 130 us
  Pallas kernels  128 us (98%)
  local copies, waits for them, and re-layouts  1.51 us (1%)
    pallas_call x1, Pallas kernels, shards(): lax.cond(shift_lon[0] <= 6, call(0), call(1), shift_lat, shift_lon, flat(...  128 us

profile of v3, /device:TPU:1, one launch (start us, length us, event | category | flops | bytes accessed | tf_op | source)
XLA Modules:
  0.0 130.1 jit_solution(1216336446963277631)
XLA Ops:
  0.7 0.0 copy-start
  0.7 0.0 copy-start.1
  0.7 0.7 copy-done
  1.3 0.0 copy-done.1
  1.4 127.9 %conditional.1 = (bf16[144,1024]{1,0:T(8,128)(2,1)S(1)}) conditional(s32[]{:T(128)} %bitcast, (s32[1]{0:T(128)}, s32[1]{0:T(128)}, bf16[1152,128]{1,0:T(8,128)(2,1)}, bf16[1152,128]{1,0:T(8,128)(2,1)}, bf16[1152,128]{1,0:T(8,128)(2,1)}, /*index=5*/bf16[1152,128]{1,0:T(8,128)(2,1)}, f32[1,1024]{1,0:T(1,128)S(1)}, bf16[32,1024]{1,0:T(8,128)(2,1)}, ...), branch_computations={%region_0.0_spmd, %region_1.0_spmd} | conditional | flops 6000000000 | bytes 8000008 | solution.py:560
  1.4 127.9 %columns_east.1 = bf16[144,1024]{1,0:T(8,128)(2,1)S(1)} custom-call(s32[1]{0:T(128)} %get-tuple-element.68.slat, s32[1]{0:T(128)} %get-tuple-element.69.slon, bf16[1152,128]{1,0:T(8,128)(2,1)} %get-tuple-element.70.tok, bf16[1152,128]{1,0:T(8,128)(2,1)} %get-tuple-element.71.qry, bf16[1152,128]{1,0:T(8,128)(2,1)} %get-tuple-element.72.key, ...), custom_call_target="tpu_custom_call" | custom-call | flops 6000000000 | bytes 8000000 | tf_op jit(solution)/shard_map/cond/branch_1_fun/columns_east/pallas_call | solution.py:560
  129.2 0.8 reshape.59
Async XLA Ops:
  0.7 0.7 copy-start
  0.7 0.7 copy-start.1

commit v4 on v3

--- a/solution.py
+++ b/solution.py
@@ -336,11 +336,10 @@
         sbuf[pl.ds(g * 4, 4)] = stacked(
             ybuf[pl.ds(pl.multiple_of(g * GROUP_ROWS, 16), GROUP_ROWS)]
         )
-    rbuf[me] = sbuf[me]
-    for i in range(GROUPS):
-        g = group(i)
         for o in range(4):
-            if not (i == 0 and o == 0):
+            if i == 0 and o == 0:
+                rbuf[me] = sbuf[me]
+            else:
                 a2a(g * 4 + lax.rem(sm + o, 4)).start()
 
     def ag(way, i):
@@ -356,8 +355,7 @@
         )
 
     def forward(i):
-        ag(0, i).wait_recv()
-        ag(1, i).wait_recv()
+        ag(i % 2, i).wait_recv()
         fw(i).start()
 
     def ffn(plane, count, half):
@@ -382,6 +380,10 @@
 
     def halves(half):
         return range(4 * half, 4 * half + 4)
+
+    def others(half):
+        for i in halves(half):
+            ag(1 - i % 2, i).wait_recv()
 
     def direct(i):
         ra(1 - i % 2, i).start()
@@ -434,6 +436,7 @@
         if i == 5:
             ffn(0, 1, 0)
         if i == 6:
+            others(0)
             ffn(1, 2, 0)
             for k in halves(0):
                 direct(k)
@@ -443,6 +446,7 @@
     for i in halves(0):
         relayed(i)
     relay(1)
+    others(1)
     ffn(1, 2, 1)
     for i in halves(1):
         direct(i)

time: 130 us -> 130 us (level)
  no operation moved by 1% of the time
where the time goes in v4:
time: 130 us
  Pallas kernels  127 us (98%)
  local copies, waits for them, and re-layouts  1.51 us (1%)
    pallas_call x1, Pallas kernels, shards(): lax.cond(shift_lon[0] <= 6, call(0), call(1), shift_lat, shift_lon, flat(...  127 us

profile of v4, /device:TPU:1, one launch (start us, length us, event | category | flops | bytes accessed | tf_op | source)
XLA Modules:
  0.0 129.6 jit_solution(9926498405944180405)
XLA Ops:
  0.7 0.0 copy-start
  0.7 0.0 copy-start.1
  0.7 0.7 copy-done
  1.3 0.0 copy-done.1
  1.4 127.4 %conditional.1 = (bf16[144,1024]{1,0:T(8,128)(2,1)S(1)}) conditional(s32[]{:T(128)} %bitcast, (s32[1]{0:T(128)}, s32[1]{0:T(128)}, bf16[1152,128]{1,0:T(8,128)(2,1)}, bf16[1152,128]{1,0:T(8,128)(2,1)}, bf16[1152,128]{1,0:T(8,128)(2,1)}, /*index=5*/bf16[1152,128]{1,0:T(8,128)(2,1)}, f32[1,1024]{1,0:T(1,128)S(1)}, bf16[32,1024]{1,0:T(8,128)(2,1)}, ...), branch_computations={%region_0.0_spmd, %region_1.0_spmd} | conditional | flops 6000000000 | bytes 8000008 | solution.py:564
  1.4 127.4 %columns_east.1 = bf16[144,1024]{1,0:T(8,128)(2,1)S(1)} custom-call(s32[1]{0:T(128)} %get-tuple-element.68.slat, s32[1]{0:T(128)} %get-tuple-element.69.slon, bf16[1152,128]{1,0:T(8,128)(2,1)} %get-tuple-element.70.tok, bf16[1152,128]{1,0:T(8,128)(2,1)} %get-tuple-element.71.qry, bf16[1152,128]{1,0:T(8,128)(2,1)} %get-tuple-element.72.key, ...), custom_call_target="tpu_custom_call" | custom-call | flops 6000000000 | bytes 8000000 | tf_op jit(solution)/shard_map/cond/branch_1_fun/columns_east/pallas_call | solution.py:564
  128.8 0.8 reshape.59
Async XLA Ops:
  0.7 0.7 copy-start
  0.7 0.7 copy-start.1
